TPU v7x, 512 devices: a whole 4x8x8 slice. The times are simulated.
512 devices in a mesh: ens: 2 (over core), lat: 32 (over z, x), chan: 8 (over y).
Axes of the slice: x: 4, y: 8, z: 8, core: 2. Of those that a mesh axis runs over, the one named last changes fastest.
Arguments:
- field: bfloat16 [2, 384, 128, 256], P('ens', 'chan', 'lat'), may hold values from -6 to 6
- cotangent: bfloat16 [2, 384, 128, 256], P('ens', 'chan', 'lat'), may hold values from -6 to 6
- spec_weight: float32 [2, 64, 384], P(None, None, 'chan'), may hold values from -8 to 8
- disco_coef: float32 [128, 9], replicated, may hold values from -2 to 2
- disco_weight: float32 [9, 384], P(None, 'chan'), may hold values from -5 to 5
- disco_rows: int32 [128, 9], replicated, may hold values from 0 to 127, as said below
- disco_shift: int32 [128, 9], replicated, may hold values from -8 to 8
- w_hidden: bfloat16 [384, 768], replicated, may hold values from -0.3125 to 0.3125
- w_output: bfloat16 [768, 384], replicated, may hold values from -0.21875 to 0.21875
Outputs:
- grad_field: bfloat16 [2, 384, 128, 256], P('ens', 'chan', 'lat')
- grad_spec_weight: float32 [2, 64, 384], P(None, None, 'chan')
- grad_disco_weight: float32 [9, 384], P(None, 'chan')
- grad_w_hidden: float32 [384, 768], P('lat')
- grad_w_output: float32 [768, 384], P('lat')
Inputs may be any that keep to these rules, and one draw needn't show every extreme that they name: Entry k of row i of disco_rows names a latitude row within 2 rows of i.
All inputs are finite; a program needn't handle non-finite values.
Results may differ from a plain program's by a relative error of at most 0.013.
Values may be sent and summed in bfloat16 or wider, within the bound.
A program may use at most 64 MiB of HBM per device.

v0:
```python
import math
import jax
import jax.numpy as jnp
from jax import lax
from jax.sharding import PartitionSpec as P

HALO = 2
SHIFT = 8
norm_eps = 1e-06
inv_root_two = 0.7071067811865476
inv_root_tau = 0.3989422804014327
highest = lax.Precision.HIGHEST


def padded_2(block, sides, width):
    for axis, dim in sides:
        count = lax.axis_size(axis)
        forward = [(i, i + 1) for i in range(count - 1)]
        backward = [(target, source) for source, target in forward]
        low = lax.ppermute(
            lax.slice_in_dim(block, block.shape[dim] - width, None, axis=dim), axis, forward
        )
        high = lax.ppermute(lax.slice_in_dim(block, 0, width, axis=dim), axis, backward)
        block = jnp.concatenate([low, block, high], axis=dim)
    return block


def colatitudes(lat_count):
    return (jnp.arange(lat_count, dtype=jnp.int32).astype(jnp.float32) + 0.5) * (
        math.pi / lat_count
    )


def legendre_rows(first_order, order_count, lat_count, degree_count):
    colatitude = colatitudes(lat_count)
    cosine = jnp.cos(colatitude)
    sine_rows = jnp.sin(colatitude)
    orders = (first_order + jnp.arange(order_count, dtype=jnp.int32)).astype(jnp.float32)
    log_start = 0.5 * (
        jnp.log((2.0 * orders + 1.0) / (4.0 * math.pi))
        + lax.lgamma(orders + 0.5)
        - lax.lgamma(orders + 1.0)
        - 0.5 * math.log(math.pi)
    )
    diagonal = jnp.exp(log_start[:, None] + orders[:, None] * jnp.log(sine_rows)[None, :])

    def advance(carry, degree):
        previous, before = carry
        degree_value = degree.astype(jnp.float32)
        above = degree_value > orders
        upper_term = jnp.where(above, 4.0 * degree_value * degree_value - 1.0, 1.0)
        lower_term = jnp.where(above, degree_value * degree_value - orders * orders, 1.0)
        factor = jnp.sqrt(upper_term / lower_term)
        behind = jnp.where(
            above, (degree_value - 1.0) * (degree_value - 1.0) - orders * orders, 0.0
        )
        damping = jnp.sqrt(behind / (4.0 * (degree_value - 1.0) * (degree_value - 1.0) - 1.0))
        recurred = factor[:, None] * (cosine[None, :] * previous - damping[:, None] * before)
        current = jnp.where(
            above[:, None], recurred, jnp.where((degree_value == orders)[:, None], diagonal, 0.0)
        )
        return ((current, previous), current)

    zero_rows = jnp.zeros((order_count, lat_count), jnp.float32)
    finish, stacked = lax.scan(
        advance, (zero_rows, zero_rows), jnp.arange(degree_count, dtype=jnp.int32), unroll=True
    )
    return jnp.transpose(stacked, (1, 0, 2))


def quadrature(lat_count, lon_count):
    return 2.0 * math.pi / lon_count * (math.pi / lat_count) * jnp.sin(colatitudes(lat_count))


def lon_tables(lon_count, mode_count):
    columns = jnp.arange(lon_count, dtype=jnp.int32)
    mode_ids = jnp.arange(mode_count, dtype=jnp.int32)
    phase_ids = columns[:, None] * mode_ids[None, :] % lon_count
    angles = phase_ids.astype(jnp.float32) * (2.0 * math.pi / lon_count)
    cosine = jnp.cos(angles)
    sine_part = jnp.sin(angles)
    forward = jnp.concatenate([cosine, -sine_part], axis=1).astype(jnp.bfloat16)
    doubled = jnp.where(mode_ids == 0, 1.0, 2.0).astype(jnp.float32)[None, :]
    inverse = jnp.transpose(
        jnp.concatenate([doubled * cosine, -doubled * sine_part], axis=1)
    ).astype(jnp.bfloat16)
    return (forward, inverse)


def apply_filter(coeffs, spec_weight):
    real_weight = jnp.transpose(spec_weight[0])[:, None, :]
    imag_weight = jnp.transpose(spec_weight[1])[:, None, :]
    real_part = coeffs[:, 0]
    imag_part = coeffs[:, 1]
    return jnp.stack(
        [
            real_weight * real_part - imag_weight * imag_part,
            real_weight * imag_part + imag_weight * real_part,
        ],
        axis=1,
    )


def filter_adjoint(grads, coeffs, spec_weight):
    real_weight = jnp.transpose(spec_weight[0])[:, None, :]
    imag_weight = jnp.transpose(spec_weight[1])[:, None, :]
    grad_real = grads[:, 0]
    grad_imag = grads[:, 1]
    real_part = coeffs[:, 0]
    imag_part = coeffs[:, 1]
    weight_zero = jnp.transpose(jnp.sum(grad_real * real_part + grad_imag * imag_part, axis=1))
    weight_one = jnp.transpose(jnp.sum(grad_imag * real_part - grad_real * imag_part, axis=1))
    adjoint_coeffs = jnp.stack(
        [
            real_weight * grad_real + imag_weight * grad_imag,
            real_weight * grad_imag - imag_weight * grad_real,
        ],
        axis=1,
    )
    return (adjoint_coeffs, jnp.stack([weight_zero, weight_one], axis=0))


def mlp_backward(mixed_rows, adjoint_rows, w_hidden, w_output):
    mixed32 = mixed_rows.astype(jnp.float32)
    rscale = lax.rsqrt(jnp.mean(mixed32 * mixed32, axis=0, keepdims=True) + norm_eps)
    normed32 = mixed32 * rscale
    normed = normed32.astype(jnp.bfloat16)
    preact = lax.dot_general(
        w_hidden, normed, (((0,), (0,)), ((), ())), preferred_element_type=jnp.float32
    )
    activated = jax.nn.gelu(preact, approximate=False).astype(jnp.bfloat16)
    grad_output = lax.dot_general(
        activated, adjoint_rows, (((1,), (1,)), ((), ())), preferred_element_type=jnp.float32
    )
    grad_act = lax.dot_general(
        w_output, adjoint_rows, (((1,), (0,)), ((), ())), preferred_element_type=jnp.float32
    )
    cumulative = 0.5 * (1.0 + lax.erf(preact * inv_root_two))
    density = jnp.exp(-0.5 * preact * preact) * inv_root_tau
    grad_pre = (grad_act * (cumulative + preact * density)).astype(jnp.bfloat16)
    grad_hidden = lax.dot_general(
        normed, grad_pre, (((1,), (1,)), ((), ())), preferred_element_type=jnp.float32
    )
    grad_normed = lax.dot_general(
        w_hidden, grad_pre, (((1,), (0,)), ((), ())), preferred_element_type=jnp.float32
    )
    grad_mixed = (
        rscale * (grad_normed - normed32 * jnp.mean(grad_normed * normed32, axis=0, keepdims=True))
    ).astype(jnp.bfloat16)
    return (grad_mixed, grad_hidden, grad_output)


def to_modes(spectrum):
    return lax.all_to_all(spectrum, "lat", split_axis=3, concat_axis=1, tiled=True)


def to_bands(spectrum):
    return lax.all_to_all(spectrum, "lat", split_axis=1, concat_axis=3, tiled=True)


def wrap_lon(values, width):
    return jnp.concatenate([values[:, :, -width:], values, values[:, :, :width]], axis=2)


def disco_kernel(rows_tab, shift_tab, coef_tab, centre, disco_weight):
    row_step = rows_tab - centre[:, None] + HALO
    lon_step = shift_tab + SHIFT
    reach = jnp.arange(2 * HALO + 1, dtype=jnp.int32)
    span = jnp.arange(2 * SHIFT + 1, dtype=jnp.int32)
    onehot = (
        (row_step[:, :, None, None] == reach[None, None, :, None])
        & (lon_step[:, :, None, None] == span[None, None, None, :])
    ).astype(jnp.float32)
    kernel = jnp.einsum("rk,rkpq,kc->crpq", coef_tab, onehot, disco_weight, precision=highest)
    return (onehot, kernel)


def shards(
    field,
    cotangent,
    spec_weight,
    disco_coef,
    disco_weight,
    disco_rows,
    disco_shift,
    w_hidden,
    w_output,
):
    member = field[0]
    adjoint_member = cotangent[0]
    channels, lat_rows, lon_count = member.shape
    band_count = lax.axis_size("lat")
    lat_count = lat_rows * band_count
    mode_count = lat_count // 2
    modes_here = mode_count // band_count
    band_index = lax.axis_index("lat")
    first_row = band_index * lat_rows
    forward, inverse = lon_tables(lon_count, mode_count)
    legendre = legendre_rows(band_index * modes_here, modes_here, lat_count, mode_count)
    weighted = legendre * quadrature(lat_count, lon_count)[None, None, :]
    grad_scale = 1.0 / math.sqrt(lax.axis_size("ens") * lat_count * lon_count)
    reach_count = 2 * HALO + 1
    span_count = 2 * SHIFT + 1
    adjoint_rows = lax.all_to_all(adjoint_member, "chan", split_axis=2, concat_axis=0, tiled=True)
    spectrum = jnp.dot(
        member.reshape(channels * lat_rows, lon_count), forward, preferred_element_type=jnp.float32
    )
    spectrum = spectrum.astype(jnp.bfloat16).reshape(channels, lat_rows, 2, mode_count)
    mode_block = to_modes(spectrum)
    coeffs = jnp.einsum(
        "citm,mli->ctml", mode_block.astype(jnp.float32), weighted, precision=highest
    )
    synthesis = jnp.einsum(
        "ctml,mli->citm", apply_filter(coeffs, spec_weight), legendre, precision=highest
    ).astype(jnp.bfloat16)
    band_block = to_bands(synthesis)
    spectral = jnp.dot(
        band_block.reshape(channels * lat_rows, 2 * mode_count),
        inverse,
        preferred_element_type=jnp.float32,
    )
    spectral = spectral.reshape(channels, lat_rows, lon_count)
    global_rows = first_row + jnp.arange(lat_rows, dtype=jnp.int32)
    rows_here = lax.dynamic_slice_in_dim(disco_rows, first_row, lat_rows, 0)
    shift_here = lax.dynamic_slice_in_dim(disco_shift, first_row, lat_rows, 0)
    coef_here = lax.dynamic_slice_in_dim(disco_coef, first_row, lat_rows, 0)
    onehot_here, kernel_here = disco_kernel(
        rows_here, shift_here, coef_here, global_rows, disco_weight
    )
    padded = padded_2(member, (("lat", 1),), HALO)
    wide_field = wrap_lon(padded, SHIFT)
    disco_out = jnp.zeros((channels, lat_rows, lon_count), jnp.float32)
    for reach in range(reach_count):
        for span in range(span_count):
            window = wide_field[:, reach : reach + lat_rows, span : span + lon_count].astype(
                jnp.float32
            )
            disco_out = disco_out + kernel_here[:, :, reach, span][:, :, None] * window
    mixed_field = (spectral + disco_out).astype(jnp.bfloat16)
    mixed_rows = lax.all_to_all(mixed_field, "chan", split_axis=2, concat_axis=0, tiled=True)
    all_channels = mixed_rows.shape[0]
    row_width = mixed_rows.shape[2]
    grad_rows, grad_hidden, grad_output = mlp_backward(
        mixed_rows.reshape(all_channels, lat_rows * row_width),
        adjoint_rows.reshape(all_channels, lat_rows * row_width),
        w_hidden,
        w_output,
    )
    grad_field = lax.all_to_all(
        grad_rows.reshape(all_channels, lat_rows, row_width),
        "chan",
        split_axis=0,
        concat_axis=2,
        tiled=True,
    )
    grad_synth = lax.dot_general(
        grad_field.reshape(channels * lat_rows, lon_count),
        inverse,
        (((1,), (1,)), ((), ())),
        preferred_element_type=jnp.float32,
    )
    grad_synth = grad_synth.astype(jnp.bfloat16).reshape(channels, lat_rows, 2, mode_count)
    grad_modes = to_modes(grad_synth)
    grad_filtered = jnp.einsum(
        "citm,mli->ctml", grad_modes.astype(jnp.float32), legendre, precision=highest
    )
    grad_coeffs, filter_part = filter_adjoint(grad_filtered, coeffs, spec_weight)
    grad_spectrum = jnp.einsum("ctml,mli->citm", grad_coeffs, weighted, precision=highest).astype(
        jnp.bfloat16
    )
    grad_lines = to_bands(grad_spectrum)
    spectral_back = lax.dot_general(
        grad_lines.reshape(channels * lat_rows, 2 * mode_count),
        forward,
        (((1,), (1,)), ((), ())),
        preferred_element_type=jnp.float32,
    )
    spectral_back = spectral_back.reshape(channels, lat_rows, lon_count)
    grad_wide = grad_field.astype(jnp.float32)
    reach_sums = []
    for reach in range(reach_count):
        span_sums = []
        for span in range(span_count):
            window = wide_field[:, reach : reach + lat_rows, span : span + lon_count].astype(
                jnp.float32
            )
            span_sums.append(jnp.sum(window * grad_wide, axis=2))
        reach_sums.append(jnp.stack(span_sums, axis=2))
    inner_sum = jnp.stack(reach_sums, axis=2)
    disco_part = jnp.einsum(
        "ik,ikpq,cipq->kc", coef_here, onehot_here, inner_sum, precision=highest
    )
    rimmed = padded_2(grad_field, (("lat", 1),), HALO)
    wide_grads = wrap_lon(rimmed, SHIFT)
    ext_count = lat_rows + 2 * HALO
    ext_rows = first_row - HALO + jnp.arange(ext_count, dtype=jnp.int32)
    rows_ext = lax.dynamic_slice_in_dim(
        jnp.pad(disco_rows, ((HALO, HALO), (0, 0))), first_row, ext_count, 0
    )
    shift_ext = lax.dynamic_slice_in_dim(
        jnp.pad(disco_shift, ((HALO, HALO), (0, 0))), first_row, ext_count, 0
    )
    coef_ext = lax.dynamic_slice_in_dim(
        jnp.pad(disco_coef, ((HALO, HALO), (0, 0))), first_row, ext_count, 0
    )
    onehot_ext, kernel_ext = disco_kernel(rows_ext, shift_ext, coef_ext, ext_rows, disco_weight)
    spread = jnp.zeros((channels, lat_rows, lon_count), jnp.float32)
    for reach in range(reach_count):
        row_start = 2 * HALO - reach
        for span in range(span_count):
            col_start = 2 * SHIFT - span
            window = wide_grads[
                :, row_start : row_start + lat_rows, col_start : col_start + lon_count
            ].astype(jnp.float32)
            spread = (
                spread
                + kernel_ext[:, row_start : row_start + lat_rows, reach, span][:, :, None] * window
            )
    grad_input = (adjoint_member.astype(jnp.float32) + spectral_back + spread).astype(jnp.bfloat16)
    filter_total, disco_total = lax.psum((filter_part, disco_part), ("ens", "lat"))
    total_hidden, total_output = lax.psum((grad_hidden, grad_output), ("ens", "lat", "chan"))
    hidden_rows = total_hidden.shape[0] // band_count
    output_rows = total_output.shape[0] // band_count
    share_hidden = lax.dynamic_slice_in_dim(total_hidden, band_index * hidden_rows, hidden_rows, 0)
    share_output = lax.dynamic_slice_in_dim(total_output, band_index * output_rows, output_rows, 0)
    return (
        grad_input[None],
        filter_total,
        disco_total * grad_scale,
        share_hidden * grad_scale,
        share_output * grad_scale,
    )


def solution(mesh):
    in_specs = (
        P("ens", "chan", "lat", None),
        P("ens", "chan", "lat", None),
        P(None, None, "chan"),
        P(),
        P(None, "chan"),
        P(),
        P(),
        P(),
        P(),
    )
    out_specs = (
        P("ens", "chan", "lat", None),
        P(None, None, "chan"),
        P(None, "chan"),
        P("lat", None),
        P("lat", None),
    )
    return jax.shard_map(shards, mesh=mesh, in_specs=in_specs, out_specs=out_specs, check_vma=False)
```

profile of v0, /device:TPU:256, one launch (start us, length us, event | category | flops | bytes accessed | tf_op | source)
XLA Modules:
  0.0 485.7 jit_solution(5748793667730272015)
XLA Ops:
  9.7 9.9 %all-to-all-start = ((bf16[32,2,384]{2,1,0:T(2,128)(2,1)}), bf16[32,2,384]{2,1,0:T(2,128)(2,1)S(1)}, u32[]{:S(2)}, u32[]{:S(2)}) async-start(bf16[32,2,384]{2,1,0:T(2,128)(2,1)} %reshape.55196), calls=%async_computation | async-start | bytes 98304 | tf_op jit(solution)/shard_map/all_to_all | solution.py:154
  19.6 3.4 collective-permute-start
  23.0 5.8 %collective-permute-start.1 = (bf16[48,2,256]{2,0,1:T(8,128)(2,1)S(1)}, bf16[48,2,256]{2,0,1:T(8,128)(2,1)S(1)}, u32[]{:S(2)}, u32[]{:S(2)}) collective-permute-start(bf16[48,2,256]{2,0,1:T(8,128)(2,1)S(1)} %get-tuple-element.536), channel_id=1, source_target_pairs={{8,0},{16,8},{24,16},{32,24},{40,32},{48,40},{56,48},{64,56},{72,6... | collective-permute-start | bytes 147464 | tf_op jit(solution)/shard_map/ppermute | solution.py:23
  89.2 7.4 %all-to-all-start.1 = ((bf16[32,2,384]{2,1,0:T(2,128)(2,1)}), bf16[32,2,384]{2,1,0:T(2,128)(2,1)S(1)}, u32[]{:S(2)}, u32[]{:S(2)}) async-start(bf16[32,2,384]{2,1,0:T(2,128)(2,1)} %reshape.55198), calls=%async_computation.1 | async-start | bytes 98304 | tf_op jit(solution)/shard_map/all_to_all | solution.py:158
  96.8 4.9 %all-to-all-done.1 = bf16[32,2,384]{2,1,0:T(2,128)(2,1)S(1)} async-done(((bf16[32,2,384]{2,1,0:T(2,128)(2,1)}), bf16[32,2,384]{2,1,0:T(2,128)(2,1)S(1)}, u32[]{:S(2)}, u32[]{:S(2)}) %all-to-all-start.1) | async-done | bytes 49184 | tf_op jit(solution)/shard_map/all_to_all | solution.py:158
  101.7 7.1 %all-to-all-start.3 = ((bf16[8,2,3072]{2,1,0:T(2,128)(2,1)}), bf16[8,2,3072]{2,1,0:T(2,128)(2,1)S(1)}, u32[]{:S(2)}, u32[]{:S(2)}) async-start(bf16[8,2,3072]{2,1,0:T(2,128)(2,1)} %reshape.55202), calls=%async_computation.3 | async-start | bytes 196608 | tf_op jit(solution)/shard_map/all_to_all | solution.py:204
  109.5 6.0 %fusion.2 = bf16[48,4,256]{2,0,1:T(8,128)(2,1)S(1)} fusion(bf16[48,4,128]{0,2,1:T(8,128)(2,1)S(1)} %bitcast.623, bf16[48,4,256]{2,0,1:T(8,128)(2,1)S(1)} %bitcast.596, f32[48,4]{0,1:T(4,128)S(1)} %bitcast.820, f32[48,4]{0,1:T(4,128)S(1)} %bitcast.821, f32[48,4]{0,1:T(4,128)S(1)} %bitcast.822, f32[48,4]{0,1:T(4,128)S(1)} %bitcast.823, ...), kind=kOutput, calls=%fused_computation.173 | convolution fusion | flops 25493504 | bytes 8339200 | tf_op jit(solution)/shard_map/dot_general | solution.py:217
  117.6 6.4 %all-to-all-start.2 = ((bf16[8,2,3072]{2,1,0:T(2,128)(2,1)}), bf16[8,2,3072]{2,1,0:T(2,128)(2,1)S(1)}, u32[]{:S(2)}, u32[]{:S(2)}) async-start(bf16[8,2,3072]{2,1,0:T(2,128)(2,1)} %reshape.55200), calls=%async_computation.2 | async-start | bytes 196608 | tf_op jit(solution)/shard_map/all_to_all | solution.py:240
  125.2 7.5 %all-to-all-done.2 = bf16[8,2,3072]{2,1,0:T(2,128)(2,1)S(1)} async-done(((bf16[8,2,3072]{2,1,0:T(2,128)(2,1)}), bf16[8,2,3072]{2,1,0:T(2,128)(2,1)S(1)}, u32[]{:S(2)}, u32[]{:S(2)}) %all-to-all-start.2) | async-done | bytes 98336 | tf_op jit(solution)/shard_map/all_to_all | solution.py:240
  134.6 2.0 fusion.24
  138.8 3.4 all-to-all-start.4
  142.5 1.5 fusion.613
  144.0 6.9 %all-to-all-done.4 = bf16[8,2,3072]{2,1,0:T(2,128)(2,1)S(1)} async-done(((bf16[8,2,3072]{2,1,0:T(2,128)(2,1)}), bf16[8,2,3072]{2,1,0:T(2,128)(2,1)S(1)}, u32[]{:S(2)}, u32[]{:S(2)}) %all-to-all-start.4) | async-done | bytes 98336 | tf_op jit(solution)/shard_map/all_to_all | solution.py:249
  152.1 1.1 fusion.210
  153.2 1.2 fusion.219
  155.5 1.2 fusion.218
  158.3 8.6 %all-to-all-start.5 = ((bf16[32,2,384]{2,1,0:T(2,128)(2,1)}), bf16[32,2,384]{2,1,0:T(2,128)(2,1)S(1)}, u32[]{:S(2)}, u32[]{:S(2)}) async-start(bf16[32,2,384]{2,1,0:T(2,128)(2,1)} %reshape.55206), calls=%async_computation.5 | async-start | bytes 98304 | tf_op jit(solution)/shard_map/all_to_all | solution.py:154
  166.9 3.4 collective-permute-start.2
  170.3 5.8 %collective-permute-start.3 = (bf16[48,2,256]{2,0,1:T(8,128)(2,1)S(1)}, bf16[48,2,256]{2,0,1:T(8,128)(2,1)S(1)}, u32[]{:S(2)}, u32[]{:S(2)}) collective-permute-start(bf16[48,2,256]{2,0,1:T(8,128)(2,1)S(1)} %get-tuple-element.534), channel_id=1, source_target_pairs={{8,0},{16,8},{24,16},{32,24},{40,32},{48,40},{56,48},{64,56},{72,6... | collective-permute-start | bytes 147464 | tf_op jit(solution)/shard_map/ppermute | solution.py:23
  180.3 10.2 %all-to-all-start.6 = ((bf16[32,2,384]{2,1,0:T(2,128)(2,1)}), bf16[32,2,384]{2,1,0:T(2,128)(2,1)S(1)}, u32[]{:S(2)}, u32[]{:S(2)}) async-start(bf16[32,2,384]{2,1,0:T(2,128)(2,1)} %reshape.55208), calls=%async_computation.6 | async-start | bytes 98304 | tf_op jit(solution)/shard_map/all_to_all | solution.py:158
  190.5 276.9 %all-reduce.4 = (f32[2,64,48]{1,2,0:T(8,128)}, f32[9,48]{1,0:T(8,128)S(1)}) all-reduce(f32[2,64,48]{1,2,0:T(8,128)S(1)} %pad_maximum_fusion.8, f32[9,48]{1,0:T(8,128)S(1)} %convolution_bitcast_fusion.6), channel_id=1, replica_groups=mesh['ens'=2,'lat'=32,'chan'=8] {'ens','lat'}, use_global_device_ids=true, to_apply=%region_5.6 | all-reduce | flops 6576 | bytes 52608 | tf_op jit(solution)/shard_map/psum | solution.py:320
  468.7 6.5 %fusion.4 = bf16[1,48,4,256]{3,1,2,0:T(8,128)(2,1)S(1)} fusion(bf16[48,4,128]{0,2,1:T(8,128)(2,1)S(1)} %bitcast.622, bf16[48,4,256]{2,0,1:T(8,128)(2,1)S(1)} %all_to_all.100, bf16[48,8,256]{2,0,1:T(8,128)(2,1)S(1)} %get-tuple-element.539, bf16[48,8,8]{2,0,1:T(8,128)(2,1)S(1)} %get-tuple-element.520, bf16[48,8,8]{2,0,1:T(8,128)(2,1)S(1)} %get-tuple-element.519, ...), kind=kOutput, calls=%fused_computation.177 | convolution fusion | flops 37191680 | bytes 1076992 | tf_op jit(solution)/shard_map/dot_general | solution.py:272
  475.9 1.5 dynamic-slice_multiply_fusion
  477.5 1.4 dynamic-slice_multiply_fusion.1
  (449 shorter events, 37.7 us)
Async XLA Ops:
  9.7 77.4 %all-to-all-start = ((bf16[32,2,384]{2,1,0:T(2,128)(2,1)}), bf16[32,2,384]{2,1,0:T(2,128)(2,1)S(1)}, u32[]{:S(2)}, u32[]{:S(2)}) async-start(bf16[32,2,384]{2,1,0:T(2,128)(2,1)} %reshape.55196), calls=%async_computation | async-start | bytes 98304 | tf_op jit(solution)/shard_map/all_to_all | solution.py:154
  19.6 67.3 %collective-permute-start = (bf16[48,2,256]{2,0,1:T(8,128)(2,1)S(1)}, bf16[48,2,256]{2,0,1:T(8,128)(2,1)S(1)}, u32[]{:S(2)}, u32[]{:S(2)}) collective-permute-start(bf16[48,2,256]{2,0,1:T(8,128)(2,1)S(1)} %get-tuple-element.537), channel_id=1, source_target_pairs={{0,8},{8,16},{16,24},{24,32},{32,40},{40,48},{48,56},{56,64},{64,7... | collective-permute-start | bytes 147464 | tf_op jit(solution)/shard_map/ppermute | solution.py:20
  23.0 63.9 %collective-permute-start.1 = (bf16[48,2,256]{2,0,1:T(8,128)(2,1)S(1)}, bf16[48,2,256]{2,0,1:T(8,128)(2,1)S(1)}, u32[]{:S(2)}, u32[]{:S(2)}) collective-permute-start(bf16[48,2,256]{2,0,1:T(8,128)(2,1)S(1)} %get-tuple-element.536), channel_id=1, source_target_pairs={{8,0},{16,8},{24,16},{32,24},{40,32},{48,40},{56,48},{64,56},{72,6... | collective-permute-start | bytes 147464 | tf_op jit(solution)/shard_map/ppermute | solution.py:23
  89.2 12.5 %all-to-all-start.1 = ((bf16[32,2,384]{2,1,0:T(2,128)(2,1)}), bf16[32,2,384]{2,1,0:T(2,128)(2,1)S(1)}, u32[]{:S(2)}, u32[]{:S(2)}) async-start(bf16[32,2,384]{2,1,0:T(2,128)(2,1)} %reshape.55198), calls=%async_computation.1 | async-start | bytes 98304 | tf_op jit(solution)/shard_map/all_to_all | solution.py:158
  101.7 15.8 %all-to-all-start.3 = ((bf16[8,2,3072]{2,1,0:T(2,128)(2,1)}), bf16[8,2,3072]{2,1,0:T(2,128)(2,1)S(1)}, u32[]{:S(2)}, u32[]{:S(2)}) async-start(bf16[8,2,3072]{2,1,0:T(2,128)(2,1)} %reshape.55202), calls=%async_computation.3 | async-start | bytes 196608 | tf_op jit(solution)/shard_map/all_to_all | solution.py:204
  117.6 15.1 %all-to-all-start.2 = ((bf16[8,2,3072]{2,1,0:T(2,128)(2,1)}), bf16[8,2,3072]{2,1,0:T(2,128)(2,1)S(1)}, u32[]{:S(2)}, u32[]{:S(2)}) async-start(bf16[8,2,3072]{2,1,0:T(2,128)(2,1)} %reshape.55200), calls=%async_computation.2 | async-start | bytes 196608 | tf_op jit(solution)/shard_map/all_to_all | solution.py:240
  138.8 12.0 %all-to-all-start.4 = ((bf16[8,2,3072]{2,1,0:T(2,128)(2,1)}), bf16[8,2,3072]{2,1,0:T(2,128)(2,1)S(1)}, u32[]{:S(2)}, u32[]{:S(2)}) async-start(bf16[8,2,3072]{2,1,0:T(2,128)(2,1)} %reshape.55204), calls=%async_computation.4 | async-start | bytes 196608 | tf_op jit(solution)/shard_map/all_to_all | solution.py:249
  142.2 333.7 %all-reduce.7.cloned.1.call-start = ((), (), s32[]{:S(2)}) async-start(), calls=%async_computation.7 | async-start | bytes 4718592 | tf_op jit(solution)/shard_map/psum | solution.py:321
  158.3 19.9 %all-to-all-start.5 = ((bf16[32,2,384]{2,1,0:T(2,128)(2,1)}), bf16[32,2,384]{2,1,0:T(2,128)(2,1)S(1)}, u32[]{:S(2)}, u32[]{:S(2)}) async-start(bf16[32,2,384]{2,1,0:T(2,128)(2,1)} %reshape.55206), calls=%async_computation.5 | async-start | bytes 98304 | tf_op jit(solution)/shard_map/all_to_all | solution.py:154
  166.9 11.1 %collective-permute-start.2 = (bf16[48,2,256]{2,0,1:T(8,128)(2,1)S(1)}, bf16[48,2,256]{2,0,1:T(8,128)(2,1)S(1)}, u32[]{:S(2)}, u32[]{:S(2)}) collective-permute-start(bf16[48,2,256]{2,0,1:T(8,128)(2,1)S(1)} %get-tuple-element.535), channel_id=1, source_target_pairs={{0,8},{8,16},{16,24},{24,32},{32,40},{40,48},{48,56},{56,64},{64,7... | collective-permute-start | bytes 147464 | tf_op jit(solution)/shard_map/ppermute | solution.py:20
  170.3 7.8 %collective-permute-start.3 = (bf16[48,2,256]{2,0,1:T(8,128)(2,1)S(1)}, bf16[48,2,256]{2,0,1:T(8,128)(2,1)S(1)}, u32[]{:S(2)}, u32[]{:S(2)}) collective-permute-start(bf16[48,2,256]{2,0,1:T(8,128)(2,1)S(1)} %get-tuple-element.534), channel_id=1, source_target_pairs={{8,0},{16,8},{24,16},{32,24},{40,32},{48,40},{56,48},{64,56},{72,6... | collective-permute-start | bytes 147464 | tf_op jit(solution)/shard_map/ppermute | solution.py:23
  178.8 289.6 %copy-start.7 = (f32[48,4,1,1]{0,3,2,1:T(1,128)S(1)}, f32[48,4,1,1]{0,3,2,1:T(1,128)}, u32[]{:S(2)}) copy-start(f32[48,4,1,1]{0,3,2,1:T(1,128)} %get-tuple-element.400) | copy-start | bytes 2308
  178.8 289.6 %copy-start.8 = (f32[48,4,1,1]{0,3,2,1:T(1,128)S(1)}, f32[48,4,1,1]{0,3,2,1:T(1,128)}, u32[]{:S(2)}) copy-start(f32[48,4,1,1]{0,3,2,1:T(1,128)} %get-tuple-element.401) | copy-start | bytes 2308
  178.8 289.6 %copy-start.9 = (f32[48,4,1,1]{0,3,2,1:T(1,128)S(1)}, f32[48,4,1,1]{0,3,2,1:T(1,128)}, u32[]{:S(2)}) copy-start(f32[48,4,1,1]{0,3,2,1:T(1,128)} %get-tuple-element.402) | copy-start | bytes 2308
  178.8 289.6 %copy-start.10 = (f32[48,4,1,1]{0,3,2,1:T(1,128)S(1)}, f32[48,4,1,1]{0,3,2,1:T(1,128)}, u32[]{:S(2)}) copy-start(f32[48,4,1,1]{0,3,2,1:T(1,128)} %get-tuple-element.403) | copy-start | bytes 2308
  178.8 289.6 %copy-start.11 = (f32[48,4,1,1]{0,3,2,1:T(1,128)S(1)}, f32[48,4,1,1]{0,3,2,1:T(1,128)}, u32[]{:S(2)}) copy-start(f32[48,4,1,1]{0,3,2,1:T(1,128)} %get-tuple-element.404) | copy-start | bytes 2308
  178.8 289.6 %copy-start.12 = (f32[48,4,1,1]{0,3,2,1:T(1,128)S(1)}, f32[48,4,1,1]{0,3,2,1:T(1,128)}, u32[]{:S(2)}) copy-start(f32[48,4,1,1]{0,3,2,1:T(1,128)} %get-tuple-element.405) | copy-start | bytes 2308
  178.8 289.6 %copy-start.13 = (f32[48,4,1,1]{0,3,2,1:T(1,128)S(1)}, f32[48,4,1,1]{0,3,2,1:T(1,128)}, u32[]{:S(2)}) copy-start(f32[48,4,1,1]{0,3,2,1:T(1,128)} %get-tuple-element.406) | copy-start | bytes 2308
  178.8 289.6 %copy-start.14 = (f32[48,4,1,1]{0,3,2,1:T(1,128)S(1)}, f32[48,4,1,1]{0,3,2,1:T(1,128)}, u32[]{:S(2)}) copy-start(f32[48,4,1,1]{0,3,2,1:T(1,128)} %get-tuple-element.407) | copy-start | bytes 2308
  178.9 289.6 %copy-start.15 = (f32[48,4,1,1]{0,3,2,1:T(1,128)S(1)}, f32[48,4,1,1]{0,3,2,1:T(1,128)}, u32[]{:S(2)}) copy-start(f32[48,4,1,1]{0,3,2,1:T(1,128)} %get-tuple-element.408) | copy-start | bytes 2308
  178.9 289.6 %copy-start.16 = (f32[48,4,1,1]{0,3,2,1:T(1,128)S(1)}, f32[48,4,1,1]{0,3,2,1:T(1,128)}, u32[]{:S(2)}) copy-start(f32[48,4,1,1]{0,3,2,1:T(1,128)} %get-tuple-element.409) | copy-start | bytes 2308
  178.9 289.6 %copy-start.17 = (f32[48,4,1,1]{0,3,2,1:T(1,128)S(1)}, f32[48,4,1,1]{0,3,2,1:T(1,128)}, u32[]{:S(2)}) copy-start(f32[48,4,1,1]{0,3,2,1:T(1,128)} %get-tuple-element.410) | copy-start | bytes 2308
  178.9 289.6 %copy-start.18 = (f32[48,4,1,1]{0,3,2,1:T(1,128)S(1)}, f32[48,4,1,1]{0,3,2,1:T(1,128)}, u32[]{:S(2)}) copy-start(f32[48,4,1,1]{0,3,2,1:T(1,128)} %get-tuple-element.411) | copy-start | bytes 2308
  180.3 287.7 %all-to-all-start.6 = ((bf16[32,2,384]{2,1,0:T(2,128)(2,1)}), bf16[32,2,384]{2,1,0:T(2,128)(2,1)S(1)}, u32[]{:S(2)}, u32[]{:S(2)}) async-start(bf16[32,2,384]{2,1,0:T(2,128)(2,1)} %reshape.55208), calls=%async_computation.6 | async-start | bytes 98304 | tf_op jit(solution)/shard_map/all_to_all | solution.py:158
  (71 other events, 7585.3 us)
Sparse Core Ops, SparseCore 0:
  148.1 279.6 all-reduce.6
where the time goes:
time: 487 us; the launch traced here: 486 us
  blocking collectives  277 us (57%)
  starting transfers between devices  71.5 us (15%)
  between operations  58.2 us (12%)
  local copies, waits for them, and re-layouts  24.1 us (5%)
  matrix products  20.6 us (4%)
  waiting for transfers between devices  20.2 us (4%)
  other arithmetic  14.3 us (3%)
    psum x1, blocking collectives, shards(): lax.psum((filter_part, disco_part), ('ens', 'lat'))  277 us
    all_to_all x2, starting transfers between devices, to_modes(): lax.all_to_all(spectrum, 'lat', split_axis=3, concat_axis=1, tiled=True)  18.5 us
    all_to_all x2, starting transfers between devices, to_bands(): lax.all_to_all(spectrum, 'lat', split_axis=1, concat_axis=3, tiled=True)  17.6 us
    ppermute x2, starting transfers between devices, padded_2(): lax.ppermute(lax.slice_in_dim(block, 0, width, axis=dim), axis, backward)  11.6 us
  transfers between devices with their start and end apart: 12, of which 4 were waited for; matrix products, arithmetic and copies ran while one was open for 9% of the time, Pallas kernels for 0%

commit v1 on v0

--- a/solution.py
+++ b/solution.py
@@ -317,7 +317,11 @@
                 + kernel_ext[:, row_start : row_start + lat_rows, reach, span][:, :, None] * window
             )
     grad_input = (adjoint_member.astype(jnp.float32) + spectral_back + spread).astype(jnp.bfloat16)
-    filter_total, disco_total = lax.psum((filter_part, disco_part), ("ens", "lat"))
+
+    def pipes_try_all(mine_x, device_axis, peer_axis):
+        return lax.psum(lax.psum(mine_x, device_axis), peer_axis)
+
+    filter_total, disco_total = pipes_try_all((filter_part, disco_part), "ens", "lat")
     total_hidden, total_output = lax.psum((grad_hidden, grad_output), ("ens", "lat", "chan"))
     hidden_rows = total_hidden.shape[0] // band_count
     output_rows = total_output.shape[0] // band_count

time: 487 us -> 444 us (0.912)
  the two profiles are of different devices: /device:TPU:256 before, /device:TPU:1 now
where the time goes in v1:
time: 444 us; the launch traced here: 443 us
  waiting for transfers between devices  133 us (30%)
  blocking collectives  127 us (29%)
  starting transfers between devices  65.2 us (15%)
  between operations  58 us (13%)
  local copies, waits for them, and re-layouts  24.1 us (5%)
  matrix products  20.6 us (5%)
  other arithmetic  14.3 us (3%)
    psum x2, blocking collectives, pipes_try_all(): return lax.psum(lax.psum(mine_x, device_axis), peer_axis)  127 us
    psum x1, waiting for transfers between devices, shards(): lax.psum((grad_hidden, grad_output), ('ens', 'lat', 'chan'))  110 us
    all_to_all x2, starting transfers between devices, to_bands(): lax.all_to_all(spectrum, 'lat', split_axis=1, concat_axis=3, tiled=True)  21.8 us
    all_to_all x2, starting transfers between devices, to_modes(): lax.all_to_all(spectrum, 'lat', split_axis=3, concat_axis=1, tiled=True)  17.6 us
    unnamed x193, local copies, waits for them, and re-layouts  9.26 us
  transfers between devices with their start and end apart: 12, of which 6 were waited for; matrix products, arithmetic and copies ran while one was open for 10% of the time, Pallas kernels for 0%

profile of v1, /device:TPU:1, one launch (start us, length us, event | category | flops | bytes accessed | tf_op | source)
XLA Modules:
  0.0 442.6 jit_solution(13903442897942134869)
XLA Ops:
  9.7 13.7 %all-to-all-start = ((bf16[32,2,384]{2,1,0:T(2,128)(2,1)}), bf16[32,2,384]{2,1,0:T(2,128)(2,1)S(1)}, u32[]{:S(2)}, u32[]{:S(2)}) async-start(bf16[32,2,384]{2,1,0:T(2,128)(2,1)} %reshape.55196), calls=%async_computation | async-start | bytes 98304 | tf_op jit(solution)/shard_map/all_to_all | solution.py:154
  23.5 3.1 collective-permute-start
  26.6 1.3 collective-permute-start.1
  88.2 11.0 %all-to-all-start.1 = ((bf16[32,2,384]{2,1,0:T(2,128)(2,1)}), bf16[32,2,384]{2,1,0:T(2,128)(2,1)S(1)}, u32[]{:S(2)}, u32[]{:S(2)}) async-start(bf16[32,2,384]{2,1,0:T(2,128)(2,1)} %reshape.55198), calls=%async_computation.1 | async-start | bytes 98304 | tf_op jit(solution)/shard_map/all_to_all | solution.py:158
  99.4 8.6 %all-to-all-done.1 = bf16[32,2,384]{2,1,0:T(2,128)(2,1)S(1)} async-done(((bf16[32,2,384]{2,1,0:T(2,128)(2,1)}), bf16[32,2,384]{2,1,0:T(2,128)(2,1)S(1)}, u32[]{:S(2)}, u32[]{:S(2)}) %all-to-all-start.1) | async-done | bytes 49184 | tf_op jit(solution)/shard_map/all_to_all | solution.py:158
  107.9 6.8 %all-to-all-start.3 = ((bf16[8,2,3072]{2,1,0:T(2,128)(2,1)}), bf16[8,2,3072]{2,1,0:T(2,128)(2,1)S(1)}, u32[]{:S(2)}, u32[]{:S(2)}) async-start(bf16[8,2,3072]{2,1,0:T(2,128)(2,1)} %reshape.55202), calls=%async_computation.3 | async-start | bytes 196608 | tf_op jit(solution)/shard_map/all_to_all | solution.py:204
  115.5 5.9 %fusion.2 = bf16[48,4,256]{2,0,1:T(8,128)(2,1)S(1)} fusion(bf16[48,4,128]{0,2,1:T(8,128)(2,1)S(1)} %bitcast.623, bf16[48,4,256]{2,0,1:T(8,128)(2,1)S(1)} %bitcast.596, f32[48,4]{0,1:T(4,128)S(1)} %bitcast.820, f32[48,4]{0,1:T(4,128)S(1)} %bitcast.821, f32[48,4]{0,1:T(4,128)S(1)} %bitcast.822, f32[48,4]{0,1:T(4,128)S(1)} %bitcast.823, ...), kind=kOutput, calls=%fused_computation.173 | convolution fusion | flops 25493504 | bytes 8339200 | tf_op jit(solution)/shard_map/dot_general | solution.py:217
  122.6 6.6 %all-to-all-start.2 = ((bf16[8,2,3072]{2,1,0:T(2,128)(2,1)}), bf16[8,2,3072]{2,1,0:T(2,128)(2,1)S(1)}, u32[]{:S(2)}, u32[]{:S(2)}) async-start(bf16[8,2,3072]{2,1,0:T(2,128)(2,1)} %reshape.55200), calls=%async_computation.2 | async-start | bytes 196608 | tf_op jit(solution)/shard_map/all_to_all | solution.py:240
  130.6 6.3 %all-to-all-done.2 = bf16[8,2,3072]{2,1,0:T(2,128)(2,1)S(1)} async-done(((bf16[8,2,3072]{2,1,0:T(2,128)(2,1)}), bf16[8,2,3072]{2,1,0:T(2,128)(2,1)S(1)}, u32[]{:S(2)}, u32[]{:S(2)}) %all-to-all-start.2) | async-done | bytes 98336 | tf_op jit(solution)/shard_map/all_to_all | solution.py:240
  138.8 2.0 fusion.24
  143.0 3.4 all-to-all-start.4
  146.7 1.4 fusion.613
  148.1 5.7 %all-to-all-done.4 = bf16[8,2,3072]{2,1,0:T(2,128)(2,1)S(1)} async-done(((bf16[8,2,3072]{2,1,0:T(2,128)(2,1)}), bf16[8,2,3072]{2,1,0:T(2,128)(2,1)S(1)}, u32[]{:S(2)}, u32[]{:S(2)}) %all-to-all-start.4) | async-done | bytes 98336 | tf_op jit(solution)/shard_map/all_to_all | solution.py:249
  161.3 3.9 all-to-all-start.5
  165.2 3.0 collective-permute-start.2
  168.2 1.3 collective-permute-start.3
  171.5 2.1 collective-permute-done.3
  176.0 10.8 %all-to-all-start.6 = ((bf16[32,2,384]{2,1,0:T(2,128)(2,1)}), bf16[32,2,384]{2,1,0:T(2,128)(2,1)S(1)}, u32[]{:S(2)}, u32[]{:S(2)}) async-start(bf16[32,2,384]{2,1,0:T(2,128)(2,1)} %reshape.55208), calls=%async_computation.6 | async-start | bytes 98304 | tf_op jit(solution)/shard_map/all_to_all | solution.py:158
  186.8 11.8 %all-reduce.5 = (f32[2,64,48]{1,2,0:T(8,128)S(1)}, f32[9,48]{1,0:T(8,128)S(1)}) all-reduce(f32[2,64,48]{1,2,0:T(8,128)S(1)} %pad_maximum_fusion.8, f32[9,48]{1,0:T(8,128)S(1)} %convolution_bitcast_fusion.6), channel_id=1, replica_groups=mesh['ens'=2,'lat'=32,'chan'=8] {'ens'}, use_global_device_ids=true, to_apply=%region_5.6 | all-reduce | flops 6576 | bytes 52608 | tf_op jit(solution)/shard_map/psum | solution.py:322
  198.6 115.7 %all-reduce.4 = (f32[2,64,48]{1,2,0:T(8,128)}, f32[9,48]{1,0:T(8,128)S(1)}) all-reduce(f32[2,64,48]{1,2,0:T(8,128)S(1)} %get-tuple-element.136, f32[9,48]{1,0:T(8,128)S(1)} %get-tuple-element.137), channel_id=1, replica_groups=mesh['ens'=2,'lat'=32,'chan'=8] {'lat'}, use_global_device_ids=true, to_apply=%region_6.7 | all-reduce | flops 6576 | bytes 52608 | tf_op jit(solution)/shard_map/psum | solution.py:322
  315.5 6.5 %fusion.4 = bf16[1,48,4,256]{3,1,2,0:T(8,128)(2,1)S(1)} fusion(bf16[48,4,128]{0,2,1:T(8,128)(2,1)S(1)} %bitcast.622, bf16[48,4,256]{2,0,1:T(8,128)(2,1)S(1)} %all_to_all.100, bf16[48,8,256]{2,0,1:T(8,128)(2,1)S(1)} %get-tuple-element.541, bf16[48,8,8]{2,0,1:T(8,128)(2,1)S(1)} %get-tuple-element.522, bf16[48,8,8]{2,0,1:T(8,128)(2,1)S(1)} %get-tuple-element.521, ...), kind=kOutput, calls=%fused_computation.177 | convolution fusion | flops 37191680 | bytes 1076992 | tf_op jit(solution)/shard_map/dot_general | solution.py:272
  322.8 110.1 %all-reduce.8.cloned.1.call-done = (f32[384,768]{1,0:T(8,128)}, f32[768,384]{1,0:T(8,128)}) async-done(((f32[384,768]{1,0:T(8,128)}, f32[768,384]{1,0:T(8,128)}), (f32[384,768]{1,0:T(8,128)}, f32[768,384]{1,0:T(8,128)})) %all-reduce.8.cloned.1.call-update) | async-done | bytes 2359312 | tf_op jit(solution)/shard_map/psum | solution.py:325
  432.9 1.5 dynamic-slice_multiply_fusion
  434.4 1.4 dynamic-slice_multiply_fusion.1
  (450 shorter events, 40.6 us)
Async XLA Ops:
  9.7 76.3 %all-to-all-start = ((bf16[32,2,384]{2,1,0:T(2,128)(2,1)}), bf16[32,2,384]{2,1,0:T(2,128)(2,1)S(1)}, u32[]{:S(2)}, u32[]{:S(2)}) async-start(bf16[32,2,384]{2,1,0:T(2,128)(2,1)} %reshape.55196), calls=%async_computation | async-start | bytes 98304 | tf_op jit(solution)/shard_map/all_to_all | solution.py:154
  23.5 62.4 %collective-permute-start = (bf16[48,2,256]{2,0,1:T(8,128)(2,1)S(1)}, bf16[48,2,256]{2,0,1:T(8,128)(2,1)S(1)}, u32[]{:S(2)}, u32[]{:S(2)}) collective-permute-start(bf16[48,2,256]{2,0,1:T(8,128)(2,1)S(1)} %get-tuple-element.539), channel_id=1, source_target_pairs={{0,8},{8,16},{16,24},{24,32},{32,40},{40,48},{48,56},{56,64},{64,7... | collective-permute-start | bytes 147464 | tf_op jit(solution)/shard_map/ppermute | solution.py:20
  26.6 59.3 %collective-permute-start.1 = (bf16[48,2,256]{2,0,1:T(8,128)(2,1)S(1)}, bf16[48,2,256]{2,0,1:T(8,128)(2,1)S(1)}, u32[]{:S(2)}, u32[]{:S(2)}) collective-permute-start(bf16[48,2,256]{2,0,1:T(8,128)(2,1)S(1)} %get-tuple-element.538), channel_id=1, source_target_pairs={{8,0},{16,8},{24,16},{32,24},{40,32},{48,40},{56,48},{64,56},{72,6... | collective-permute-start | bytes 147464 | tf_op jit(solution)/shard_map/ppermute | solution.py:23
  88.2 19.7 %all-to-all-start.1 = ((bf16[32,2,384]{2,1,0:T(2,128)(2,1)}), bf16[32,2,384]{2,1,0:T(2,128)(2,1)S(1)}, u32[]{:S(2)}, u32[]{:S(2)}) async-start(bf16[32,2,384]{2,1,0:T(2,128)(2,1)} %reshape.55198), calls=%async_computation.1 | async-start | bytes 98304 | tf_op jit(solution)/shard_map/all_to_all | solution.py:158
  107.9 14.7 %all-to-all-start.3 = ((bf16[8,2,3072]{2,1,0:T(2,128)(2,1)}), bf16[8,2,3072]{2,1,0:T(2,128)(2,1)S(1)}, u32[]{:S(2)}, u32[]{:S(2)}) async-start(bf16[8,2,3072]{2,1,0:T(2,128)(2,1)} %reshape.55202), calls=%async_computation.3 | async-start | bytes 196608 | tf_op jit(solution)/shard_map/all_to_all | solution.py:204
  122.6 14.2 %all-to-all-start.2 = ((bf16[8,2,3072]{2,1,0:T(2,128)(2,1)}), bf16[8,2,3072]{2,1,0:T(2,128)(2,1)S(1)}, u32[]{:S(2)}, u32[]{:S(2)}) async-start(bf16[8,2,3072]{2,1,0:T(2,128)(2,1)} %reshape.55200), calls=%async_computation.2 | async-start | bytes 196608 | tf_op jit(solution)/shard_map/all_to_all | solution.py:240
  143.0 10.9 %all-to-all-start.4 = ((bf16[8,2,3072]{2,1,0:T(2,128)(2,1)}), bf16[8,2,3072]{2,1,0:T(2,128)(2,1)S(1)}, u32[]{:S(2)}, u32[]{:S(2)}) async-start(bf16[8,2,3072]{2,1,0:T(2,128)(2,1)} %reshape.55204), calls=%async_computation.4 | async-start | bytes 196608 | tf_op jit(solution)/shard_map/all_to_all | solution.py:249
  146.4 286.5 %all-reduce.8.cloned.1.call-start = ((), (), s32[]{:S(2)}) async-start(), calls=%async_computation.7 | async-start | bytes 4718592 | tf_op jit(solution)/shard_map/psum | solution.py:325
  161.3 12.6 %all-to-all-start.5 = ((bf16[32,2,384]{2,1,0:T(2,128)(2,1)}), bf16[32,2,384]{2,1,0:T(2,128)(2,1)S(1)}, u32[]{:S(2)}, u32[]{:S(2)}) async-start(bf16[32,2,384]{2,1,0:T(2,128)(2,1)} %reshape.55206), calls=%async_computation.5 | async-start | bytes 98304 | tf_op jit(solution)/shard_map/all_to_all | solution.py:154
  165.2 6.3 %collective-permute-start.2 = (bf16[48,2,256]{2,0,1:T(8,128)(2,1)S(1)}, bf16[48,2,256]{2,0,1:T(8,128)(2,1)S(1)}, u32[]{:S(2)}, u32[]{:S(2)}) collective-permute-start(bf16[48,2,256]{2,0,1:T(8,128)(2,1)S(1)} %get-tuple-element.537), channel_id=1, source_target_pairs={{0,8},{8,16},{16,24},{24,32},{32,40},{40,48},{48,56},{56,64},{64,7... | collective-permute-start | bytes 147464 | tf_op jit(solution)/shard_map/ppermute | solution.py:20
  168.2 5.3 %collective-permute-start.3 = (bf16[48,2,256]{2,0,1:T(8,128)(2,1)S(1)}, bf16[48,2,256]{2,0,1:T(8,128)(2,1)S(1)}, u32[]{:S(2)}, u32[]{:S(2)}) collective-permute-start(bf16[48,2,256]{2,0,1:T(8,128)(2,1)S(1)} %get-tuple-element.536), channel_id=1, source_target_pairs={{8,0},{16,8},{24,16},{32,24},{40,32},{48,40},{56,48},{64,56},{72,6... | collective-permute-start | bytes 147464 | tf_op jit(solution)/shard_map/ppermute | solution.py:23
  174.5 140.8 %copy-start.7 = (f32[48,4,1,1]{0,3,2,1:T(1,128)S(1)}, f32[48,4,1,1]{0,3,2,1:T(1,128)}, u32[]{:S(2)}) copy-start(f32[48,4,1,1]{0,3,2,1:T(1,128)} %get-tuple-element.402) | copy-start | bytes 2308
  174.5 140.8 %copy-start.8 = (f32[48,4,1,1]{0,3,2,1:T(1,128)S(1)}, f32[48,4,1,1]{0,3,2,1:T(1,128)}, u32[]{:S(2)}) copy-start(f32[48,4,1,1]{0,3,2,1:T(1,128)} %get-tuple-element.403) | copy-start | bytes 2308
  174.5 140.8 %copy-start.9 = (f32[48,4,1,1]{0,3,2,1:T(1,128)S(1)}, f32[48,4,1,1]{0,3,2,1:T(1,128)}, u32[]{:S(2)}) copy-start(f32[48,4,1,1]{0,3,2,1:T(1,128)} %get-tuple-element.404) | copy-start | bytes 2308
  174.5 140.8 %copy-start.10 = (f32[48,4,1,1]{0,3,2,1:T(1,128)S(1)}, f32[48,4,1,1]{0,3,2,1:T(1,128)}, u32[]{:S(2)}) copy-start(f32[48,4,1,1]{0,3,2,1:T(1,128)} %get-tuple-element.405) | copy-start | bytes 2308
  174.5 140.8 %copy-start.11 = (f32[48,4,1,1]{0,3,2,1:T(1,128)S(1)}, f32[48,4,1,1]{0,3,2,1:T(1,128)}, u32[]{:S(2)}) copy-start(f32[48,4,1,1]{0,3,2,1:T(1,128)} %get-tuple-element.406) | copy-start | bytes 2308
  174.5 140.8 %copy-start.12 = (f32[48,4,1,1]{0,3,2,1:T(1,128)S(1)}, f32[48,4,1,1]{0,3,2,1:T(1,128)}, u32[]{:S(2)}) copy-start(f32[48,4,1,1]{0,3,2,1:T(1,128)} %get-tuple-element.407) | copy-start | bytes 2308
  174.5 140.8 %copy-start.13 = (f32[48,4,1,1]{0,3,2,1:T(1,128)S(1)}, f32[48,4,1,1]{0,3,2,1:T(1,128)}, u32[]{:S(2)}) copy-start(f32[48,4,1,1]{0,3,2,1:T(1,128)} %get-tuple-element.408) | copy-start | bytes 2308
  174.5 140.8 %copy-start.14 = (f32[48,4,1,1]{0,3,2,1:T(1,128)S(1)}, f32[48,4,1,1]{0,3,2,1:T(1,128)}, u32[]{:S(2)}) copy-start(f32[48,4,1,1]{0,3,2,1:T(1,128)} %get-tuple-element.409) | copy-start | bytes 2308
  174.5 140.8 %copy-start.15 = (f32[48,4,1,1]{0,3,2,1:T(1,128)S(1)}, f32[48,4,1,1]{0,3,2,1:T(1,128)}, u32[]{:S(2)}) copy-start(f32[48,4,1,1]{0,3,2,1:T(1,128)} %get-tuple-element.410) | copy-start | bytes 2308
  174.5 140.8 %copy-start.16 = (f32[48,4,1,1]{0,3,2,1:T(1,128)S(1)}, f32[48,4,1,1]{0,3,2,1:T(1,128)}, u32[]{:S(2)}) copy-start(f32[48,4,1,1]{0,3,2,1:T(1,128)} %get-tuple-element.411) | copy-start | bytes 2308
  174.6 140.8 %copy-start.17 = (f32[48,4,1,1]{0,3,2,1:T(1,128)S(1)}, f32[48,4,1,1]{0,3,2,1:T(1,128)}, u32[]{:S(2)}) copy-start(f32[48,4,1,1]{0,3,2,1:T(1,128)} %get-tuple-element.412) | copy-start | bytes 2308
  174.6 140.8 %copy-start.18 = (f32[48,4,1,1]{0,3,2,1:T(1,128)S(1)}, f32[48,4,1,1]{0,3,2,1:T(1,128)}, u32[]{:S(2)}) copy-start(f32[48,4,1,1]{0,3,2,1:T(1,128)} %get-tuple-element.413) | copy-start | bytes 2308
  176.0 138.8 %all-to-all-start.6 = ((bf16[32,2,384]{2,1,0:T(2,128)(2,1)}), bf16[32,2,384]{2,1,0:T(2,128)(2,1)S(1)}, u32[]{:S(2)}, u32[]{:S(2)}) async-start(bf16[32,2,384]{2,1,0:T(2,128)(2,1)} %reshape.55208), calls=%async_computation.6 | async-start | bytes 98304 | tf_op jit(solution)/shard_map/all_to_all | solution.py:158
  (71 other events, 4580.8 us)
Sparse Core Ops, SparseCore 0:
  152.3 280.4 all-reduce.7
